TPU v7x, 128 devices: a whole 4x4x4 slice. The times are simulated.
128 devices in a mesh: lb: 16 (over z_lo, y, core), rb: 8 (over x, z_hi).
Axes of the slice: x: 4, y: 4, z: 4 (z_hi: 2, z_lo: 2; z = z_hi * 2 + z_lo), core: 2. Of those that a mesh axis runs over, the one named last changes fastest.
Arguments:
- wavefunction: bfloat16 [3072, 4, 3072], P('lb', None, 'rb'), may hold values from -6 to 6
- left_environment: bfloat16 [8, 2048, 3072], P(None, 'lb'), may hold values from -0.109375 to 0.109375
- operator_left: float32 [8, 8, 2, 2], replicated, may hold values from -1.5 to 1.5
- operator_right: float32 [8, 8, 2, 2], replicated, may hold values from -1.5 to 1.5
- right_environment: bfloat16 [8, 3072, 3072], P(None, 'rb', 'lb'), may hold values from -0.0546875 to 0.0546875
- row_sector: int32 [16], replicated, may hold values from 0 to 7, never falling along the last dimension, each value on 1 to 4 neighbouring positions
Outputs:
- applied_state: bfloat16 [2048, 4, 3072], P('lb', None, 'rb')
- density: float32 [2048, 2048], P('lb', 'rb')
Inputs may be any that keep to these rules, and one draw needn't show every extreme that they name: `row_sector`: entry t is the sector of output rows t * 128 to (t + 1) * 128 - 1. Entries never fall along t; each sector holds 1 to 4 tiles, and one holds exactly 4.
All inputs are finite; a program needn't handle non-finite values.
Results may differ from a plain program's by a relative error of at most 0.013.
Values may be sent and summed in bfloat16 or wider, within the bound.
A program may use at most 128 MiB of HBM per device.

v0:
```python
import math
import jax
import jax.numpy as jnp
from jax import lax
from jax.sharding import Mesh
from jax.sharding import PartitionSpec as P

BOND_WIDTH = 3072
SECTOR_TILES = 4
RB = ("rb_0", "rb_1")


def shifted(value, axis, by):
    devices = lax.axis_size(axis)
    pairs = [(i, i + by) for i in range(devices) if 0 <= i + by < devices]
    return lax.ppermute(value, axis, pairs)


def summed_rows(value, axes, dim):
    for axis in axes:
        value = lax.psum_scatter(value, axis, scatter_dimension=dim, tiled=True)
    return value


def split_up(value, dim, devices):
    before, after = (value.shape[:dim], value.shape[dim + 1 :])
    return jnp.moveaxis(value.reshape(*before, devices, -1, *after), dim, 0)


def sent_and_summed(value, axis, dim):
    parts = split_up(value, dim, lax.axis_size(axis))
    arrived = lax.all_to_all(parts, axis, split_axis=0, concat_axis=0, tiled=True)
    return arrived.astype(jnp.float32).sum(axis=0)


def combine_operators(operator_left, operator_right):
    channels = operator_left.shape[0]
    joined = jnp.einsum(
        "aups,uvqt->avpqst", operator_left, operator_right, precision=lax.Precision.HIGHEST
    )
    return joined.reshape(channels, channels, 4, 4)


def label_at(labels, position):
    matches = jnp.arange(labels.shape[0], dtype=jnp.int32) == position
    return (jnp.sum(jnp.where(matches, labels, 0)), jnp.any(matches))


def tile_gram(left_tile, right_tile):
    return lax.dot_general(
        left_tile, right_tile, (((1,), (1,)), ((), ())), preferred_element_type=jnp.float32
    )


def fetch_tile(own_tile, offset):
    return shifted(own_tile, "lb", -offset)


def shards(
    wavefunction, left_environment, operator_left, operator_right, right_environment, row_sector
):
    channels, row_count, full_bond = left_environment.shape
    local_right = wavefunction.shape[2]
    left_matrix = left_environment.reshape(channels * row_count, full_bond)
    rows_piece = lax.all_gather(wavefunction, "lb", axis=0, tiled=True)
    flat_piece = rows_piece.reshape(rows_piece.shape[0], 4 * local_right)
    left_part = jnp.dot(left_matrix, flat_piece, preferred_element_type=jnp.float32)
    left_part = left_part.reshape(channels, row_count, 4, local_right)
    combined = combine_operators(operator_left, operator_right)
    mixed_part = jnp.einsum(
        "avyx,alxr->lyvr", combined, left_part, precision=lax.Precision.HIGHEST
    ).astype(jnp.bfloat16)
    mixed_matrix = mixed_part.reshape(row_count * 4, channels * local_right)
    columns_piece = lax.all_gather(right_environment, "lb", axis=2, tiled=True)
    flat_piece = columns_piece.reshape(channels * local_right, columns_piece.shape[2])
    partial_value = jnp.dot(mixed_matrix, flat_piece, preferred_element_type=jnp.float32)
    summed = summed_rows(partial_value.astype(jnp.bfloat16), RB, 1).astype(jnp.float32)
    applied = summed.astype(jnp.bfloat16).reshape(row_count, 4, summed.shape[1])
    own_tile = applied.reshape(row_count, 4 * summed.shape[1])
    own_index = lax.axis_index("lb")
    tile_count = lax.axis_size("lb")
    reach_tiles = SECTOR_TILES - 1
    own_label = label_at(row_sector, own_index)[0]
    buffer = jnp.zeros((row_count, (tile_count + 2 * reach_tiles) * row_count), jnp.float32)

    def place_block(buffer, gram_block, offset):
        mate_index = own_index + offset
        mate_label, inside = label_at(row_sector, mate_index)
        keep_block = jnp.logical_and(inside, mate_label == own_label)
        gram_block = jnp.where(keep_block, gram_block, jnp.float32(0.0))
        column_start = (mate_index + reach_tiles) * row_count
        return lax.dynamic_update_slice(buffer, gram_block, (jnp.int32(0), column_start))

    buffer = place_block(buffer, tile_gram(own_tile, own_tile), 0)
    for distance in range(1, SECTOR_TILES):
        gram_block = tile_gram(own_tile, fetch_tile(own_tile, distance))
        buffer = place_block(buffer, gram_block, distance)
        returned = shifted(gram_block.astype(jnp.bfloat16), "lb", distance).astype(gram_block.dtype)
        buffer = place_block(buffer, returned.T, -distance)
    full_rows = buffer[:, reach_tiles * row_count : (reach_tiles + tile_count) * row_count]
    density = sent_and_summed(full_rows.astype(jnp.bfloat16), RB, 1) * (
        1.0 / math.sqrt(4.0 * BOND_WIDTH)
    )
    return (applied, density)


def solution(mesh):
    torus = Mesh(mesh.devices.reshape(mesh.shape["lb"], 4, 2), ("lb", "rb_0", "rb_1"))
    in_specs = (P("lb", None, RB), P(None, "lb", None), P(), P(), P(None, RB, "lb"), P())
    out_specs = (P("lb", None, RB), P("lb", RB))
    return jax.shard_map(
        shards, mesh=torus, in_specs=in_specs, out_specs=out_specs, check_vma=False
    )
```

profile of v0, /device:TPU:1, one launch (start us, length us, event | category | flops | bytes accessed | tf_op | source)
XLA Modules:
  0.0 340.6 jit_solution(16183151076118569877)
XLA Ops:
  7.2 0.7 all-gather.3.cloned.1.call-update
  8.0 3.0 copy.27
  11.0 1.1 convolution_bitcast_fusion
  12.2 0.7 copy.25
  12.9 57.6 %all-gather.3.cloned.1.call-done = bf16[3072,4,384]{2,1,0:T(4,128)(2,1)} async-done(((bf16[192,4,384]{2,1,0:T(4,128)(2,1)}), bf16[3072,4,384]{2,1,0:T(4,128)(2,1)}) %all-gather.3.cloned.1.call-update) | async-done | bytes 9437200 | tf_op jit(solution)/shard_map/all_gather | solution.py:65
  70.5 15.5 %copy.41 = bf16[3072,4,384]{0,2,1:T(8,128)(2,1)} copy(bf16[3072,4,384]{2,1,0:T(4,128)(2,1)} %all-gather.3.cloned.1.call-done) | data formatting | bytes 18874368 | tf_op jit(solution)/shard_map/reshape | solution.py:66
  85.9 15.1 %fusion = f32[8,128,4,384]{3,0,2,1:T(8,128)S(1)} fusion(bf16[3072,4,384]{0,2,1:T(8,128)(2,1)} %copy.41, bf16[8,128,3072,1]{2,1,0,3:T(8,128)(2,1)} %bitcast.62), kind=kOutput, calls=%fused_computation | convolution fusion | flops 9663676416 | bytes 22020096 | tf_op jit(solution)/shard_map/dot_general | solution.py:67
  101.1 5.7 %bitcast_convert_fusion = bf16[128,384,8,4]{1,2,3,0:T(8,128)(2,1)S(1)} fusion(f32[8,8,4,4,1]{1,0,3,2,4:T(8,128)S(1)} %bitcast.60, f32[8,128,4,384]{3,0,2,1:T(8,128)S(1)} %fusion), kind=kOutput, calls=%fused_computation.4 | convolution fusion | flops 605552640 | bytes 9441280 | tf_op jit(solution)/shard_map/avyx,alxr->lyvr/dot_general | solution.py:70
  106.8 0.7 copy.49
  107.5 67.1 %all-gather.5.cloned.1.call-done = bf16[8,384,3072]{1,0,2:T(8,128)(2,1)} async-done(((bf16[8,384,192]{1,0,2:T(8,128)(2,1)}), bf16[8,384,3072]{1,0,2:T(8,128)(2,1)}) %all-gather.5.cloned.1.call-update) | async-done | bytes 18874384 | tf_op jit(solution)/shard_map/all_gather | solution.py:74
  174.6 24.0 %copy.28 = bf16[8,384,3072]{2,1,0:T(8,128)(2,1)} copy(bf16[8,384,3072]{1,0,2:T(8,128)(2,1)} %all-gather.5.cloned.1.call-done) | data formatting | bytes 37748736 | tf_op jit(solution)/shard_map/all_gather | solution.py:74
  198.6 15.1 %convolution_convert_fusion = bf16[512,3072]{1,0:T(8,128)(2,1)} fusion(bf16[512,3072]{1,0:T(8,128)(2,1)S(1)} %bitcast.57, bf16[3072,3072]{1,0:T(8,128)(2,1)} %bitcast.55), kind=kOutput, calls=%fused_computation.6 | convolution fusion | flops 9665249280 | bytes 25165824 | tf_op jit(solution)/shard_map/dot_general | solution.py:76
  213.8 38.6 %reduce-scatter.5.cloned.1.call-done = bf16[512,768]{1,0:T(8,128)(2,1)} async-done(((bf16[512,3072]{1,0:T(8,128)(2,1)}), bf16[512,768]{1,0:T(8,128)(2,1)}) %reduce-scatter.5.cloned.1.call-update) | async-done | bytes 786448 | tf_op jit(solution)/shard_map/reduce_scatter | solution.py:21
  252.4 2.3 copy.47
  254.8 21.5 %reduce-scatter.7.cloned.1.call-done = bf16[384,512]{1,0:T(8,128)(2,1)} async-done(((bf16[768,512]{1,0:T(8,128)(2,1)}), bf16[384,512]{1,0:T(8,128)(2,1)}) %reduce-scatter.7.cloned.1.call-update) | async-done | bytes 393232
  276.2 1.2 copy.48
  277.7 2.6 collective-permute-start
  281.5 0.7 fusion.16
  284.2 1.3 collective-permute-start.2
  285.6 0.9 fusion.7
  287.1 3.3 collective-permute-start.1
  290.5 0.6 compare_reduce_fusion.4
  295.5 1.3 collective-permute-start.4
  297.4 4.2 %collective-permute-start.3 = (bf16[128,128]{0,1:T(8,128)(2,1)S(1)}, bf16[128,128]{0,1:T(8,128)(2,1)S(1)}, u32[]{:S(2)}, u32[]{:S(2)}) collective-permute-start(bf16[128,128]{0,1:T(8,128)(2,1)S(1)} %get-tuple-element.14), channel_id=1, source_target_pairs={{0,16},{8,24},{16,32},{24,40},{32,48},{40,56},{48,64},{56,72},{64,... | collective-permute-start | bytes 98312 | tf_op jit(solution)/shard_map/ppermute | solution.py:16
  301.6 0.6 compare_reduce_fusion.2
  306.9 8.5 %collective-permute-start.5 = (bf16[128,128]{0,1:T(8,128)(2,1)S(1)}, bf16[128,128]{0,1:T(8,128)(2,1)S(1)}, u32[]{:S(2)}, u32[]{:S(2)}) collective-permute-start(bf16[128,128]{0,1:T(8,128)(2,1)S(1)} %get-tuple-element.16), channel_id=1, source_target_pairs={{0,24},{8,32},{16,40},{24,48},{32,56},{40,64},{48,72},{56,80},{64,... | collective-permute-start | bytes 98312 | tf_op jit(solution)/shard_map/ppermute | solution.py:16
  315.4 0.6 compare_reduce_fusion
  318.2 0.8 slice.7
  319.0 4.0 %all-to-all-start = ((bf16[8,128,256]{1,2,0:T(8,128)(2,1)}), bf16[8,128,256]{1,2,0:T(8,128)(2,1)S(1)}, u32[]{:S(2)}, u32[]{:S(2)}) async-start(bf16[8,128,256]{1,2,0:T(8,128)(2,1)} %bitcast.20), calls=%async_computation.1 | async-start | bytes 1048576 | tf_op jit(solution)/shard_map/all_to_all | solution.py:32
  323.0 0.8 reshape.31
  323.8 9.3 %all-to-all-done = bf16[8,128,256]{1,2,0:T(8,128)(2,1)S(1)} async-done(((bf16[8,128,256]{1,2,0:T(8,128)(2,1)}), bf16[8,128,256]{1,2,0:T(8,128)(2,1)S(1)}, u32[]{:S(2)}, u32[]{:S(2)}) %all-to-all-start) | async-done | bytes 524320 | tf_op jit(solution)/shard_map/all_to_all | solution.py:32
  333.3 0.8 copy.32
  (41 shorter events, 4.9 us)
Async XLA Ops:
  7.2 3.9 %copy-start = (f32[8,8,2,2]{1,3,2,0:T(2,128)S(1)}, f32[8,8,2,2]{1,3,2,0:T(2,128)}, u32[]{:S(2)}) copy-start(f32[8,8,2,2]{1,3,2,0:T(2,128)} %param.8) | copy-start | bytes 3076
  7.2 63.3 %all-gather.3.cloned.1.call-start = ((), (), s32[]{:S(2)}) async-start(), calls=%async_computation.3 | async-start | bytes 10027008 | tf_op jit(solution)/shard_map/all_gather | solution.py:65
  7.9 166.7 %all-gather.5.cloned.1.call-start = ((), (), s32[]{:S(2)}) async-start(), calls=%async_computation.4 | async-start | bytes 20054016 | tf_op jit(solution)/shard_map/all_gather | solution.py:74
  11.0 241.5 %reduce-scatter.5.cloned.1.call-start = ((), (), s32[]{:S(2)}) async-start(), calls=%async_computation.5 | async-start | bytes 3932160 | tf_op jit(solution)/shard_map/reduce_scatter | solution.py:21
  85.9 15.2 %copy-start.2 = (f32[8,8,2,2,2,2]{1,0,5,4,3,2:T(8,128)S(1)}, f32[8,8,2,2,2,2]{1,0,5,4,3,2:T(8,128)}, u32[]{:S(2)}) copy-start(f32[8,8,2,2,2,2]{1,0,5,4,3,2:T(8,128)} %copy.25) | copy-start | bytes 12292
  213.7 67.8 %copy-start.3 = (s32[16]{0:T(128)S(1)}, s32[16]{0:T(128)}, u32[]{:S(2)}) copy-start(s32[16]{0:T(128)} %param.11) | copy-start | bytes 196
  213.7 120.3 %copy-start.1 = (f32[8,8,2,2]{1,3,2,0:T(2,128)S(1)}, f32[8,8,2,2]{1,3,2,0:T(2,128)}, u32[]{:S(2)}) copy-start(f32[8,8,2,2]{1,3,2,0:T(2,128)} %param.8) | copy-start | bytes 3076
  213.7 62.5 %reduce-scatter.7.cloned.1.call-start = ((), (), s32[]{:S(2)}) async-start(), calls=%async_computation.6 | async-start | bytes 1179648
  277.7 9.1 %collective-permute-start = (bf16[128,1536]{1,0:T(8,128)(2,1)S(1)}, bf16[128,1536]{1,0:T(8,128)(2,1)S(1)}, u32[]{:S(2)}, u32[]{:S(2)}) collective-permute-start(bf16[128,1536]{1,0:T(8,128)(2,1)S(1)} %reshape_reshape.3), channel_id=1, source_target_pairs={{8,0},{16,8},{24,16},{32,24},{40,32},{48,40},{56,48},{64,56},{72,6... | collective-permute-start | bytes 1179656 | tf_op jit(solution)/shard_map/ppermute | solution.py:16
  284.2 13.0 %collective-permute-start.2 = (bf16[128,1536]{1,0:T(8,128)(2,1)S(1)}, bf16[128,1536]{1,0:T(8,128)(2,1)S(1)}, u32[]{:S(2)}, u32[]{:S(2)}) collective-permute-start(bf16[128,1536]{1,0:T(8,128)(2,1)S(1)} %reshape_reshape.3), channel_id=1, source_target_pairs={{16,0},{24,8},{32,16},{40,24},{48,32},{56,40},{64,48},{72,56},{80,... | collective-permute-start | bytes 1179656 | tf_op jit(solution)/shard_map/ppermute | solution.py:16
  287.1 9.7 %collective-permute-start.1 = (bf16[128,128]{0,1:T(8,128)(2,1)S(1)}, bf16[128,128]{0,1:T(8,128)(2,1)S(1)}, u32[]{:S(2)}, u32[]{:S(2)}) collective-permute-start(bf16[128,128]{0,1:T(8,128)(2,1)S(1)} %get-tuple-element.12), channel_id=1, source_target_pairs={{0,8},{8,16},{16,24},{24,32},{32,40},{40,48},{48,56},{56,64},{64,7... | collective-permute-start | bytes 98312 | tf_op jit(solution)/shard_map/ppermute | solution.py:16
  295.5 11.1 %collective-permute-start.4 = (bf16[128,1536]{1,0:T(8,128)(2,1)S(1)}, bf16[128,1536]{1,0:T(8,128)(2,1)S(1)}, u32[]{:S(2)}, u32[]{:S(2)}) collective-permute-start(bf16[128,1536]{1,0:T(8,128)(2,1)S(1)} %reshape_reshape.3), channel_id=1, source_target_pairs={{24,0},{32,8},{40,16},{48,24},{56,32},{64,40},{72,48},{80,56},{88,... | collective-permute-start | bytes 1179656 | tf_op jit(solution)/shard_map/ppermute | solution.py:16
  297.4 9.1 %collective-permute-start.3 = (bf16[128,128]{0,1:T(8,128)(2,1)S(1)}, bf16[128,128]{0,1:T(8,128)(2,1)S(1)}, u32[]{:S(2)}, u32[]{:S(2)}) collective-permute-start(bf16[128,128]{0,1:T(8,128)(2,1)S(1)} %get-tuple-element.14), channel_id=1, source_target_pairs={{0,16},{8,24},{16,32},{24,40},{32,48},{40,56},{48,64},{56,72},{64,... | collective-permute-start | bytes 98312 | tf_op jit(solution)/shard_map/ppermute | solution.py:16
  306.9 11.1 %collective-permute-start.5 = (bf16[128,128]{0,1:T(8,128)(2,1)S(1)}, bf16[128,128]{0,1:T(8,128)(2,1)S(1)}, u32[]{:S(2)}, u32[]{:S(2)}) collective-permute-start(bf16[128,128]{0,1:T(8,128)(2,1)S(1)} %get-tuple-element.16), channel_id=1, source_target_pairs={{0,24},{8,32},{16,40},{24,48},{32,56},{40,64},{48,72},{56,80},{64,... | collective-permute-start | bytes 98312 | tf_op jit(solution)/shard_map/ppermute | solution.py:16
  319.0 14.2 %all-to-all-start = ((bf16[8,128,256]{1,2,0:T(8,128)(2,1)}), bf16[8,128,256]{1,2,0:T(8,128)(2,1)S(1)}, u32[]{:S(2)}, u32[]{:S(2)}) async-start(bf16[8,128,256]{1,2,0:T(8,128)(2,1)} %bitcast.20), calls=%async_computation.1 | async-start | bytes 1048576 | tf_op jit(solution)/shard_map/all_to_all | solution.py:32
Sparse Core Ops, SparseCore 0:
  9.7 60.7 all-gather.2
  72.2 102.3 all-gather.4
  213.8 38.5 reduce-scatter.4
  254.9 21.3 reduce-scatter.6
where the time goes:
time: 342 us; the launch traced here: 341 us
  waiting for transfers between devices  195 us (57%)
  local copies, waits for them, and re-layouts  50.6 us (15%)
  matrix products  38.8 us (11%)
  starting transfers between devices  25.3 us (7%)
  between operations  25.3 us (7%)
  other arithmetic  5.29 us (2%)
    all_gather x1, waiting for transfers between devices, shards(): columns_piece = lax.all_gather(right_environment, 'lb', axis=2, tiled=True)  67.1 us
    all_gather x1, waiting for transfers between devices, shards(): rows_piece = lax.all_gather(wavefunction, 'lb', axis=0, tiled=True)  57.6 us
    reduce_scatter x1, waiting for transfers between devices, summed_rows(): value = lax.psum_scatter(value, axis, scatter_dimension=dim, tiled=True)  38.6 us
    all_gather x1, local copies, waits for them, and re-layouts, shards(): columns_piece = lax.all_gather(right_environment, 'lb', axis=2, tiled=True)  24 us
    unnamed x5, waiting for transfers between devices  22.2 us
    ppermute x6, starting transfers between devices, shifted(): return lax.ppermute(value, axis, pairs)  21.2 us
    reshape x1, local copies, waits for them, and re-layouts, shards(): flat_piece = rows_piece.reshape(rows_piece.shape[0], 4 * local_right)  15.5 us
    dot_general x1, matrix products, shards(): jnp.dot(left_matrix, flat_piece, preferred_element_type=jnp.float32)  15.1 us
  transfers between devices with their start and end apart: 11, of which 7 were waited for; matrix products, arithmetic and copies ran while one was open for 15% of the time, Pallas kernels for 0%

commit v1 on v0

--- a/solution.py
+++ b/solution.py
@@ -71,7 +71,9 @@
         "avyx,alxr->lyvr", combined, left_part, precision=lax.Precision.HIGHEST
     ).astype(jnp.bfloat16)
     mixed_matrix = mixed_part.reshape(row_count * 4, channels * local_right)
-    columns_piece = lax.all_gather(right_environment, "lb", axis=2, tiled=True)
+    columns_piece = jnp.concatenate(
+        lax.all_to_all(jnp.stack([right_environment] * lax.axis_size("lb")), "lb", 0, 0), axis=2
+    )
     flat_piece = columns_piece.reshape(channels * local_right, columns_piece.shape[2])
     partial_value = jnp.dot(mixed_matrix, flat_piece, preferred_element_type=jnp.float32)
     summed = summed_rows(partial_value.astype(jnp.bfloat16), RB, 1).astype(jnp.float32)

time: 342 us -> 502 us (1.47)
  waiting for transfers between devices: 195 us -> 348 us
  starting transfers between devices: 25.3 us -> 32.7 us
    all_to_all x0 -> x1, waiting for transfers between devices: none -> 276 us  [shards(): lax.all_to_all(jnp.stack([right_environment] * lax.axis_size('lb')), 'lb'...]
    all_gather x1 -> x0, waiting for transfers between devices: 67.1 us -> none  [shards(): columns_piece = lax.all_gather(right_environment, 'lb', axis=2, tiled=True)]
    all_gather x1, waiting for transfers between devices: 57.6 us -> 0.01 us  [shards(): rows_piece = lax.all_gather(wavefunction, 'lb', axis=0, tiled=True)]
    all_gather x1 -> x0, local copies, waits for them, and re-layouts: 24 us -> none  [shards(): columns_piece = lax.all_gather(right_environment, 'lb', axis=2, tiled=True)]
    unnamed x13 -> x16, local copies, waits for them, and re-layouts: 7.98 us -> 25.9 us
    all_to_all x0 -> x1, starting transfers between devices: none -> 7.47 us  [shards(): lax.all_to_all(jnp.stack([right_environment] * lax.axis_size('lb')), 'lb'...]
    another operation x0 -> x1, local copies, waits for them, and re-layouts: none -> 7.04 us  [shards(): jnp.stack([right_environment] * lax.axis_size('lb'))]
    unnamed x5 -> x4, waiting for transfers between devices: 22.2 us -> 22.2 us
  transfers between devices with their start and end apart: 11 -> 11, of which waited for: 7 -> 6; matrix products, arithmetic and copies ran while one was open for 15% -> 6% of each run, Pallas kernels for 0% -> 0%
where the time goes in v1:
time: 502 us; the launch traced here: 501 us
  waiting for transfers between devices  348 us (69%)
  local copies, waits for them, and re-layouts  51.4 us (10%)
  matrix products  38.2 us (8%)
  starting transfers between devices  32.7 us (7%)
  between operations  25.3 us (5%)
  other arithmetic  5.29 us (1%)
    all_to_all x1, waiting for transfers between devices, shards(): lax.all_to_all(jnp.stack([right_environment] * lax.axis_size('lb')), 'lb'...  276 us
    reduce_scatter x1, waiting for transfers between devices, summed_rows(): value = lax.psum_scatter(value, axis, scatter_dimension=dim, tiled=True)  40 us
    unnamed x16, local copies, waits for them, and re-layouts  25.9 us
    unnamed x4, waiting for transfers between devices  22.2 us
    ppermute x6, starting transfers between devices, shifted(): return lax.ppermute(value, axis, pairs)  21.2 us
    reshape x1, local copies, waits for them, and re-layouts, shards(): flat_piece = rows_piece.reshape(rows_piece.shape[0], 4 * local_right)  15.4 us
    dot_general x1, matrix products, shards(): jnp.dot(mixed_matrix, flat_piece, preferred_element_type=jnp.float32)  15.3 us
    dot_general x1, matrix products, shards(): jnp.dot(left_matrix, flat_piece, preferred_element_type=jnp.float32)  15 us
  transfers between devices with their start and end apart: 11, of which 6 were waited for; matrix products, arithmetic and copies ran while one was open for 6% of the time, Pallas kernels for 0%

profile of v1, /device:TPU:1, one launch (start us, length us, event | category | flops | bytes accessed | tf_op | source)
XLA Modules:
  0.0 500.8 jit_solution(18230184070983939264)
XLA Ops:
  7.2 2.0 copy.28
  9.1 7.0 %stack.2 = bf16[16,8,384,192]{2,1,3,0:T(8,128)(2,1)} broadcast(bf16[8,384,192]{1,0,2:T(8,128)(2,1)S(1)} %copy.28), dimensions={1,2,3} | broadcast | bytes 20054016 | tf_op jit(solution)/shard_map/stack | solution.py:75
  16.2 7.5 %all-to-all-start = ((bf16[16,8,384,192]{2,1,3,0:T(8,128)(2,1)}), bf16[16,8,384,192]{2,1,3,0:T(8,128)(2,1)}, u32[]{:S(2)}, u32[]{:S(2)}) async-start(bf16[16,8,384,192]{2,1,3,0:T(8,128)(2,1)} %stack.2), calls=%async_computation | async-start | bytes 37748736 | tf_op jit(solution)/shard_map/all_to_all | solution.py:75
  23.7 0.7 all-gather.2.cloned.1.call-update
  24.9 0.7 copy.26
  25.6 275.9 %all-to-all-done = bf16[16,8,384,192]{2,1,3,0:T(8,128)(2,1)} async-done(((bf16[16,8,384,192]{2,1,3,0:T(8,128)(2,1)}), bf16[16,8,384,192]{2,1,3,0:T(8,128)(2,1)}, u32[]{:S(2)}, u32[]{:S(2)}) %all-to-all-start) | async-done | bytes 18874400 | tf_op jit(solution)/shard_map/all_to_all | solution.py:75
  301.5 18.9 %copy.50 = bf16[384,8,8,384]{3,1,2,0:T(8,128)(2,1)} copy(bf16[384,8,8,384]{3,2,1,0:T(8,128)(2,1)} %bitcast.34) | data formatting | bytes 37748736
  320.4 15.4 %copy.41 = bf16[3072,4,384]{0,2,1:T(8,128)(2,1)} copy(bf16[3072,4,384]{2,1,0:T(4,128)(2,1)} %all-gather.2.cloned.1.call-done) | data formatting | bytes 18874368 | tf_op jit(solution)/shard_map/reshape | solution.py:66
  335.8 15.0 %fusion = f32[8,128,4,384]{3,0,2,1:T(8,128)S(1)} fusion(bf16[3072,4,384]{0,2,1:T(8,128)(2,1)} %copy.41, bf16[8,128,3072,1]{2,1,0,3:T(8,128)(2,1)} %bitcast.67), kind=kOutput, calls=%fused_computation | convolution fusion | flops 9663676416 | bytes 22020096 | tf_op jit(solution)/shard_map/dot_general | solution.py:67
  350.9 5.7 %bitcast_convert_fusion = bf16[128,384,8,4]{1,2,3,0:T(8,128)(2,1)S(1)} fusion(f32[8,8,4,4,1]{1,0,3,2,4:T(8,128)S(1)} %bitcast.65, f32[8,128,4,384]{3,0,2,1:T(8,128)S(1)} %fusion), kind=kOutput, calls=%fused_computation.4 | convolution fusion | flops 605552640 | bytes 9441280 | tf_op jit(solution)/shard_map/avyx,alxr->lyvr/dot_general | solution.py:70
  356.5 0.7 copy.49
  357.3 15.3 %convolution_convert_fusion = bf16[512,3072]{1,0:T(8,128)(2,1)} fusion(bf16[512,3072]{1,0:T(8,128)(2,1)S(1)} %bitcast.62, bf16[3072,3072]{0,1:T(8,128)(2,1)} %bitcast.60), kind=kOutput, calls=%fused_computation.6 | convolution fusion | flops 9665249280 | bytes 25165824 | tf_op jit(solution)/shard_map/dot_general | solution.py:78
  372.7 40.0 %reduce-scatter.5.cloned.1.call-done = bf16[512,768]{1,0:T(8,128)(2,1)} async-done(((bf16[512,3072]{1,0:T(8,128)(2,1)}), bf16[512,768]{1,0:T(8,128)(2,1)}) %reduce-scatter.5.cloned.1.call-update) | async-done | bytes 786448 | tf_op jit(solution)/shard_map/reduce_scatter | solution.py:21
  412.7 2.3 copy.47
  415.0 21.5 %reduce-scatter.7.cloned.1.call-done = bf16[384,512]{1,0:T(8,128)(2,1)} async-done(((bf16[768,512]{1,0:T(8,128)(2,1)}), bf16[384,512]{1,0:T(8,128)(2,1)}) %reduce-scatter.7.cloned.1.call-update) | async-done | bytes 393232
  436.5 1.2 copy.48
  437.9 2.6 collective-permute-start
  441.8 0.7 fusion.16
  444.4 1.3 collective-permute-start.2
  445.8 0.9 fusion.7
  447.3 3.4 collective-permute-start.1
  450.7 0.6 compare_reduce_fusion.4
  455.8 1.3 collective-permute-start.4
  457.6 4.1 collective-permute-start.3
  461.8 0.6 compare_reduce_fusion.2
  467.2 8.5 %collective-permute-start.5 = (bf16[128,128]{0,1:T(8,128)(2,1)S(1)}, bf16[128,128]{0,1:T(8,128)(2,1)S(1)}, u32[]{:S(2)}, u32[]{:S(2)}) collective-permute-start(bf16[128,128]{0,1:T(8,128)(2,1)S(1)} %get-tuple-element.16), channel_id=1, source_target_pairs={{0,24},{8,32},{16,40},{24,48},{32,56},{40,64},{48,72},{56,80},{64,... | collective-permute-start | bytes 98312 | tf_op jit(solution)/shard_map/ppermute | solution.py:16
  475.7 0.6 compare_reduce_fusion
  478.4 0.8 slice.7
  479.3 4.0 all-to-all-start.1
  483.2 0.8 reshape.33
  484.1 9.3 %all-to-all-done.1 = bf16[8,128,256]{1,2,0:T(8,128)(2,1)S(1)} async-done(((bf16[8,128,256]{1,2,0:T(8,128)(2,1)}), bf16[8,128,256]{1,2,0:T(8,128)(2,1)S(1)}, u32[]{:S(2)}, u32[]{:S(2)}) %all-to-all-start.1) | async-done | bytes 524320 | tf_op jit(solution)/shard_map/all_to_all | solution.py:32
  493.5 0.8 copy.32
  (43 shorter events, 5.3 us)
Async XLA Ops:
  7.2 17.3 %copy-start = (f32[8,8,2,2]{1,3,2,0:T(2,128)S(1)}, f32[8,8,2,2]{1,3,2,0:T(2,128)}, u32[]{:S(2)}) copy-start(f32[8,8,2,2]{1,3,2,0:T(2,128)} %param.8) | copy-start | bytes 3076
  16.2 8.3 %copy-start.3 = (f32[8,8,2,2]{1,3,2,0:T(2,128)S(1)}, f32[8,8,2,2]{1,3,2,0:T(2,128)}, u32[]{:S(2)}) copy-start(f32[8,8,2,2]{1,3,2,0:T(2,128)} %param.9) | copy-start | bytes 3076
  16.2 285.3 %all-to-all-start = ((bf16[16,8,384,192]{2,1,3,0:T(8,128)(2,1)}), bf16[16,8,384,192]{2,1,3,0:T(8,128)(2,1)}, u32[]{:S(2)}, u32[]{:S(2)}) async-start(bf16[16,8,384,192]{2,1,3,0:T(8,128)(2,1)} %stack.2), calls=%async_computation | async-start | bytes 37748736 | tf_op jit(solution)/shard_map/all_to_all | solution.py:75
  23.7 296.7 %all-gather.2.cloned.1.call-start = ((), (), s32[]{:S(2)}) async-start(), calls=%async_computation.4 | async-start | bytes 10027008 | tf_op jit(solution)/shard_map/all_gather | solution.py:65
  24.4 388.3 %reduce-scatter.5.cloned.1.call-start = ((), (), s32[]{:S(2)}) async-start(), calls=%async_computation.5 | async-start | bytes 3932160 | tf_op jit(solution)/shard_map/reduce_scatter | solution.py:21
  335.8 15.0 %copy-start.2 = (f32[8,8,2,2,2,2]{1,0,5,4,3,2:T(8,128)S(1)}, f32[8,8,2,2,2,2]{1,0,5,4,3,2:T(8,128)}, u32[]{:S(2)}) copy-start(f32[8,8,2,2,2,2]{1,0,5,4,3,2:T(8,128)} %copy.26) | copy-start | bytes 12292
  372.6 69.2 %copy-start.4 = (s32[16]{0:T(128)S(1)}, s32[16]{0:T(128)}, u32[]{:S(2)}) copy-start(s32[16]{0:T(128)} %param.11) | copy-start | bytes 196
  372.6 121.6 %copy-start.1 = (f32[8,8,2,2]{1,3,2,0:T(2,128)S(1)}, f32[8,8,2,2]{1,3,2,0:T(2,128)}, u32[]{:S(2)}) copy-start(f32[8,8,2,2]{1,3,2,0:T(2,128)} %param.8) | copy-start | bytes 3076
  372.6 63.8 %reduce-scatter.7.cloned.1.call-start = ((), (), s32[]{:S(2)}) async-start(), calls=%async_computation.6 | async-start | bytes 1179648
  437.9 9.1 %collective-permute-start = (bf16[128,1536]{1,0:T(8,128)(2,1)S(1)}, bf16[128,1536]{1,0:T(8,128)(2,1)S(1)}, u32[]{:S(2)}, u32[]{:S(2)}) collective-permute-start(bf16[128,1536]{1,0:T(8,128)(2,1)S(1)} %reshape_reshape.7), channel_id=1, source_target_pairs={{8,0},{16,8},{24,16},{32,24},{40,32},{48,40},{56,48},{64,56},{72,6... | collective-permute-start | bytes 1179656 | tf_op jit(solution)/shard_map/ppermute | solution.py:16
  444.4 13.0 %collective-permute-start.2 = (bf16[128,1536]{1,0:T(8,128)(2,1)S(1)}, bf16[128,1536]{1,0:T(8,128)(2,1)S(1)}, u32[]{:S(2)}, u32[]{:S(2)}) collective-permute-start(bf16[128,1536]{1,0:T(8,128)(2,1)S(1)} %reshape_reshape.7), channel_id=1, source_target_pairs={{16,0},{24,8},{32,16},{40,24},{48,32},{56,40},{64,48},{72,56},{80,... | collective-permute-start | bytes 1179656 | tf_op jit(solution)/shard_map/ppermute | solution.py:16
  447.3 9.7 %collective-permute-start.1 = (bf16[128,128]{0,1:T(8,128)(2,1)S(1)}, bf16[128,128]{0,1:T(8,128)(2,1)S(1)}, u32[]{:S(2)}, u32[]{:S(2)}) collective-permute-start(bf16[128,128]{0,1:T(8,128)(2,1)S(1)} %get-tuple-element.12), channel_id=1, source_target_pairs={{0,8},{8,16},{16,24},{24,32},{32,40},{40,48},{48,56},{56,64},{64,7... | collective-permute-start | bytes 98312 | tf_op jit(solution)/shard_map/ppermute | solution.py:16
  455.8 11.1 %collective-permute-start.4 = (bf16[128,1536]{1,0:T(8,128)(2,1)S(1)}, bf16[128,1536]{1,0:T(8,128)(2,1)S(1)}, u32[]{:S(2)}, u32[]{:S(2)}) collective-permute-start(bf16[128,1536]{1,0:T(8,128)(2,1)S(1)} %reshape_reshape.7), channel_id=1, source_target_pairs={{24,0},{32,8},{40,16},{48,24},{56,32},{64,40},{72,48},{80,56},{88,... | collective-permute-start | bytes 1179656 | tf_op jit(solution)/shard_map/ppermute | solution.py:16
  457.6 9.1 %collective-permute-start.3 = (bf16[128,128]{0,1:T(8,128)(2,1)S(1)}, bf16[128,128]{0,1:T(8,128)(2,1)S(1)}, u32[]{:S(2)}, u32[]{:S(2)}) collective-permute-start(bf16[128,128]{0,1:T(8,128)(2,1)S(1)} %get-tuple-element.14), channel_id=1, source_target_pairs={{0,16},{8,24},{16,32},{24,40},{32,48},{40,56},{48,64},{56,72},{64,... | collective-permute-start | bytes 98312 | tf_op jit(solution)/shard_map/ppermute | solution.py:16
  467.2 11.1 %collective-permute-start.5 = (bf16[128,128]{0,1:T(8,128)(2,1)S(1)}, bf16[128,128]{0,1:T(8,128)(2,1)S(1)}, u32[]{:S(2)}, u32[]{:S(2)}) collective-permute-start(bf16[128,128]{0,1:T(8,128)(2,1)S(1)} %get-tuple-element.16), channel_id=1, source_target_pairs={{0,24},{8,32},{16,40},{24,48},{32,56},{40,64},{48,72},{56,80},{64,... | collective-permute-start | bytes 98312 | tf_op jit(solution)/shard_map/ppermute | solution.py:16
  479.3 14.2 %all-to-all-start.1 = ((bf16[8,128,256]{1,2,0:T(8,128)(2,1)}), bf16[8,128,256]{1,2,0:T(8,128)(2,1)S(1)}, u32[]{:S(2)}, u32[]{:S(2)}) async-start(bf16[8,128,256]{1,2,0:T(8,128)(2,1)} %bitcast.20), calls=%async_computation.2 | async-start | bytes 1048576 | tf_op jit(solution)/shard_map/all_to_all | solution.py:32
Sparse Core Ops, SparseCore 0:
  26.2 244.9 all-gather.1
  372.8 39.8 reduce-scatter.4
  415.1 21.3 reduce-scatter.6
